TPU v7x, 32 devices: a whole 2x2x4 slice. The times are simulated.
32 devices in a mesh: grp: 2 (over x), ad: 8 (over z, y), tp: 2 (over core).
Axes of the slice: x: 2, y: 2, z: 4, core: 2. Of those that a mesh axis runs over, the one named last changes fastest.
Arguments:
- tokens: bfloat16 [2048, 8192], P(('grp', 'ad'), 'tp'), parts along dimension 0, may hold values from -6 to 6
- row_adapter_index: int32 [2048, 1], P(('grp', 'ad')), parts along dimension 0, may hold values from 0 to 7; in each aligned block of 128 rows (0 to 127, 128 to 255, ...) at most 32 rows name the same one
- key_base_matrix: bfloat16 [8192, 1024], P('tp'), may hold values from -0.0625 to 0.0625
- adapter_down_factor: bfloat16 [16, 8192, 64], P(('grp', 'ad'), 'tp'), parts along dimension 0, may hold values from -0.0625 to 0.0625
- adapter_up_factor: bfloat16 [16, 64, 1024], P(('grp', 'ad'), None, 'tp'), parts along dimension 0, may hold values from -0.75 to 0.75
Outputs:
- keys: bfloat16 [2048, 1024], P(('grp', 'ad'), 'tp'), parts along dimension 0
There are 2 independent parts, one for each index of `grp`. A program takes and returns all parts, laid end to end along the dimension named above; an argument that names none is the same for every part. Nothing has to cross between parts.
Inputs may be any that keep to these rules, and one draw needn't show every extreme that they name: `row_adapter_index`: among the rows of one index of ad, at most 32 name the same adapter, and in every draw some adapter is named exactly 32 times by the rows of some index.
All inputs are finite; a program needn't handle non-finite values.
Results may differ from a plain program's by a relative error of at most 0.005.
Values may be sent and summed in bfloat16 or wider, within the bound.
A program may use at most 64 MiB of HBM per device.

v0:
```python
import jax
import jax.numpy as jnp
from jax import lax
from jax.sharding import PartitionSpec as P


def on_device(tokens, row_adapter_index, key_base_matrix, adapter_down_factor, adapter_up_factor):
    row_count = tokens.shape[0]
    ad_count = lax.axis_size("ad")
    capacity = max(2, 2 * row_count // ad_count)
    row_adapter = row_adapter_index[:, 0]
    one_hot = (row_adapter[:, None] == jnp.arange(ad_count, dtype=jnp.int32)[None, :]).astype(
        jnp.int32
    )
    earlier = jnp.cumsum(one_hot, axis=0) - one_hot
    slot_index = jnp.sum(earlier * one_hot, axis=1)
    position = row_adapter * capacity + slot_index
    feature_half = tokens.shape[1]
    outgoing = jnp.zeros((ad_count * capacity, feature_half), jnp.bfloat16).at[position].set(tokens)
    outgoing = outgoing.reshape(ad_count, capacity, feature_half)
    down_factor_half = adapter_down_factor[0]
    up_factor_half = adapter_up_factor[0]
    full_down = lax.all_gather(down_factor_half, "tp", axis=0, tiled=True)
    received = lax.all_to_all(outgoing, "ad", split_axis=0, concat_axis=0, tiled=True)
    item_count = received.shape[1]
    flat_rows = received.reshape(ad_count * item_count, feature_half)
    whole_rows = lax.all_gather(flat_rows, "tp", axis=1, tiled=True)
    shrunk = jnp.dot(whole_rows, full_down, preferred_element_type=jnp.float32).astype(jnp.bfloat16)
    expanded = jnp.dot(shrunk, up_factor_half, preferred_element_type=jnp.float32).astype(
        jnp.bfloat16
    )
    expanded = expanded.reshape(ad_count, item_count, up_factor_half.shape[1])
    returned = lax.all_to_all(expanded, "ad", split_axis=0, concat_axis=0, tiled=True)
    base_part = jnp.dot(tokens, key_base_matrix, preferred_element_type=jnp.float32)
    base_half = lax.psum_scatter(base_part, "tp", scatter_dimension=1, tiled=True)
    delta_rows = returned.reshape(ad_count * capacity, up_factor_half.shape[1])[position]
    return (base_half + delta_rows.astype(jnp.float32)).astype(jnp.bfloat16)


def solution(mesh):
    placed = (
        P(("grp", "ad"), "tp"),
        P(("grp", "ad"), None),
        P("tp", None),
        P(("grp", "ad"), "tp", None),
        P(("grp", "ad"), None, "tp"),
    )
    return jax.shard_map(
        on_device, mesh=mesh, in_specs=placed, out_specs=P(("grp", "ad"), "tp"), check_vma=False
    )
```

profile of v0, /device:TPU:0, one launch (start us, length us, event | category | flops | bytes accessed | tf_op | source)
XLA Modules:
  0.0 112.0 jit_solution(5768854574005919625)
XLA Ops:
  6.5 0.0 copy-start
  6.5 0.8 fusion.5
  7.3 0.2 reduce_window_sum.11
  7.5 0.8 select_reduce_fusion
  8.3 0.7 fusion.6
  9.0 0.0 copy-start.2
  9.0 4.4 %scatter_custom_fusion = bf16[256,4096]{1,0:T(8,128)(2,1)} fusion(s32[128]{0:T(128)S(1)} %fusion.6, bf16[128,4096]{1,0:T(8,128)(2,1)} %param.5, bf16[]{:T(256)} %constant.4.clone.1), kind=kCustom, calls=%fused_computation.5 | custom fusion | bytes 2097664 | tf_op jit(solution)/shard_map/scatter | solution.py:19
  13.4 7.3 %all-to-all-start = ((bf16[8,32,4096]{2,1,0:T(8,128)(2,1)}), bf16[8,32,4096]{2,1,0:T(8,128)(2,1)S(1)}, u32[]{:S(2)}, u32[]{:S(2)}) async-start(bf16[8,32,4096]{2,1,0:T(8,128)(2,1)} %bitcast.22), calls=%async_computation.1 | async-start | bytes 4194304 | tf_op jit(solution)/shard_map/all_to_all | solution.py:24
  20.6 0.0 all-gather.6.cloned.1.call-start
  20.7 0.7 all-gather.6.cloned.1.call-update
  21.4 0.0 all-gather.4.cloned.1.call-start
  21.4 47.5 %all-to-all-done = bf16[8,32,4096]{2,1,0:T(8,128)(2,1)S(1)} async-done(((bf16[8,32,4096]{2,1,0:T(8,128)(2,1)}), bf16[8,32,4096]{2,1,0:T(8,128)(2,1)S(1)}, u32[]{:S(2)}, u32[]{:S(2)}) %all-to-all-start) | async-done | bytes 2097184 | tf_op jit(solution)/shard_map/all_to_all | solution.py:24
  68.9 0.0 copy-start.1
  68.9 1.3 %copy-done.1 = bf16[8,32,4096]{2,1,0:T(8,128)(2,1)} copy-done((bf16[8,32,4096]{2,1,0:T(8,128)(2,1)}, bf16[8,32,4096]{2,1,0:T(8,128)(2,1)S(1)}, u32[]{:S(2)}) %copy-start.1) | copy-done | bytes 2097176
  70.2 0.0 all-gather.4.cloned.1.call-update
  70.2 0.0 reduce-scatter.2.cloned.1.call-start
  70.3 0.0 copy-done.2
  70.3 5.4 %fusion.7 = f32[128,1024]{1,0:T(8,128)} fusion(bf16[128,4096]{1,0:T(8,128)(2,1)S(1)} %copy-done.2, bf16[4096,1024]{1,0:T(8,128)(2,1)} %param.7), kind=kOutput, calls=%fused_computation.16 | convolution fusion | flops 1073741824 | bytes 9961472 | tf_op jit(solution)/shard_map/dot_general | solution.py:34
  75.7 0.0 reduce-scatter.2.cloned.1.call-update
  75.7 0.0 all-gather.6.cloned.1.call-done
  75.7 7.4 %all-gather.4.cloned.1.call-done = bf16[256,8192]{1,0:T(8,128)(2,1)} async-done(((bf16[256,4096]{1,0:T(8,128)(2,1)}), bf16[256,8192]{1,0:T(8,128)(2,1)}) %all-gather.4.cloned.1.call-update) | async-done | bytes 4194320 | tf_op jit(solution)/shard_map/all_gather | solution.py:27
  83.1 0.0 copy-done
  83.1 4.7 %convolution_convert_fusion = bf16[256,512]{1,0:T(8,128)(2,1)} fusion(bf16[256,8192]{1,0:T(8,128)(2,1)} %all-gather.4.cloned.1.call-done, bf16[1,8192,64]{1,2,0:T(8,128)(2,1)} %all-gather.6.cloned.1.call-done, bf16[1,64,512]{2,1,0:T(8,128)(2,1)S(1)} %copy-done), kind=kOutput, calls=%fused_computation.2 | convolution fusion | flops 285360128 | bytes 5570560 | tf_op jit(solution)/shard_map/dot_general | solution.py:29
  87.8 5.8 %all-to-all-start.1 = ((bf16[8,32,512]{2,1,0:T(8,128)(2,1)}), bf16[8,32,512]{2,1,0:T(8,128)(2,1)S(1)}, u32[]{:S(2)}, u32[]{:S(2)}) async-start(bf16[8,32,512]{2,1,0:T(8,128)(2,1)} %bitcast.7), calls=%async_computation.2 | async-start | bytes 524288 | tf_op jit(solution)/shard_map/all_to_all | solution.py:33
  93.6 9.4 %all-to-all-done.1 = bf16[8,32,512]{2,1,0:T(8,128)(2,1)S(1)} async-done(((bf16[8,32,512]{2,1,0:T(8,128)(2,1)}), bf16[8,32,512]{2,1,0:T(8,128)(2,1)S(1)}, u32[]{:S(2)}, u32[]{:S(2)}) %all-to-all-start.1) | async-done | bytes 262176 | tf_op jit(solution)/shard_map/all_to_all | solution.py:33
  102.9 0.8 gather_fusion
  103.8 0.0 reduce-scatter.2.cloned.1.call-done
  103.8 1.6 %add_convert_fusion = bf16[128,512]{1,0:T(8,128)(2,1)} fusion(f32[128,512]{1,0:T(8,128)} %reduce-scatter.2.cloned.1.call-done, bf16[128,512]{1,0:T(8,128)(2,1)S(1)} %gather_fusion), kind=kLoop, calls=%fused_computation.7 | loop fusion | flops 196608 | bytes 524288 | tf_op jit(solution)/shard_map/convert_element_type | solution.py:37
  (1 shorter events, 0.0 us)
Async XLA Ops:
  6.5 76.6 %copy-start = (bf16[1,64,512]{2,1,0:T(8,128)(2,1)S(1)}, bf16[1,64,512]{2,1,0:T(8,128)(2,1)}, u32[]{:S(2)}) copy-start(bf16[1,64,512]{2,1,0:T(8,128)(2,1)} %param.9) | copy-start | bytes 196612
  9.0 61.3 %copy-start.2 = (bf16[128,4096]{1,0:T(8,128)(2,1)S(1)}, bf16[128,4096]{1,0:T(8,128)(2,1)}, u32[]{:S(2)}) copy-start(bf16[128,4096]{1,0:T(8,128)(2,1)} %param.5) | copy-start | bytes 3145732
  13.4 55.5 %all-to-all-start = ((bf16[8,32,4096]{2,1,0:T(8,128)(2,1)}), bf16[8,32,4096]{2,1,0:T(8,128)(2,1)S(1)}, u32[]{:S(2)}, u32[]{:S(2)}) async-start(bf16[8,32,4096]{2,1,0:T(8,128)(2,1)} %bitcast.22), calls=%async_computation.1 | async-start | bytes 4194304 | tf_op jit(solution)/shard_map/all_to_all | solution.py:24
  20.6 55.1 %all-gather.6.cloned.1.call-start = ((), (), s32[]{:S(2)}) async-start(), calls=%async_computation.5 | async-start | bytes 1572864 | tf_op jit(solution)/shard_map/all_gather | solution.py:23
  21.4 61.7 %all-gather.4.cloned.1.call-start = ((), (), s32[]{:S(2)}) async-start(), calls=%async_computation.4 | async-start | bytes 6291456 | tf_op jit(solution)/shard_map/all_gather | solution.py:27
  68.9 1.3 %copy-start.1 = (bf16[8,32,4096]{2,1,0:T(8,128)(2,1)}, bf16[8,32,4096]{2,1,0:T(8,128)(2,1)S(1)}, u32[]{:S(2)}) copy-start(bf16[8,32,4096]{2,1,0:T(8,128)(2,1)S(1)} %all-to-all-done) | copy-start | bytes 6291460
  70.2 33.6 %reduce-scatter.2.cloned.1.call-start = ((), (), s32[]{:S(2)}) async-start(), calls=%async_computation.3 | async-start | bytes 786432 | tf_op jit(solution)/shard_map/reduce_scatter | solution.py:35
  87.8 15.2 %all-to-all-start.1 = ((bf16[8,32,512]{2,1,0:T(8,128)(2,1)}), bf16[8,32,512]{2,1,0:T(8,128)(2,1)S(1)}, u32[]{:S(2)}, u32[]{:S(2)}) async-start(bf16[8,32,512]{2,1,0:T(8,128)(2,1)} %bitcast.7), calls=%async_computation.2 | async-start | bytes 524288 | tf_op jit(solution)/shard_map/all_to_all | solution.py:33
Sparse Core Ops, SparseCore 0:
  23.0 10.4 all-gather.5
  70.3 12.7 all-gather.3
  85.4 9.1 reduce-scatter.1
where the time goes:
time: 112 us
  waiting for transfers between devices  65 us (58%)
  starting transfers between devices  13.2 us (12%)
  between operations  13.2 us (12%)
  matrix products  10.1 us (9%)
  local copies, waits for them, and re-layouts  6.55 us (6%)
  other arithmetic  4.07 us (4%)
    all_to_all x1, waiting for transfers between devices, on_device(): lax.all_to_all(outgoing, 'ad', split_axis=0, concat_axis=0, tiled=True)  47.5 us
    all_to_all x1, waiting for transfers between devices, on_device(): lax.all_to_all(expanded, 'ad', split_axis=0, concat_axis=0, tiled=True)  9.37 us
    all_gather x1, waiting for transfers between devices, on_device(): whole_rows = lax.all_gather(flat_rows, 'tp', axis=1, tiled=True)  7.36 us
    all_to_all x1, starting transfers between devices, on_device(): lax.all_to_all(outgoing, 'ad', split_axis=0, concat_axis=0, tiled=True)  7.28 us
    all_to_all x1, starting transfers between devices, on_device(): lax.all_to_all(expanded, 'ad', split_axis=0, concat_axis=0, tiled=True)  5.77 us
    dot_general x1, matrix products, on_device(): jnp.dot(tokens, key_base_matrix, preferred_element_type=jnp.float32)  5.41 us
    dot_general x1, matrix products, on_device(): jnp.dot(shrunk, up_factor_half, preferred_element_type=jnp.float32)  4.66 us
    scatter x1, local copies, waits for them, and re-layouts, on_device(): jnp.zeros((ad_count * capacity, feature_half), jnp.bfloat16).at[position]  4.37 us
  transfers between devices with their start and end apart: 5, of which 3 were waited for; matrix products, arithmetic and copies ran while one was open for 10% of the time, Pallas kernels for 0%

commit v1 on v0

v1 whole, which is shorter than its diff:
```python
import functools

import jax
import jax.numpy as jnp
from jax import lax
from jax.experimental import pallas as pl
from jax.experimental.pallas import tpu as pltpu
from jax.sharding import PartitionSpec as P

MESH = pl.DeviceIdType.MESH
LANES = 128
BASE_CHUNKS = 8


def flip(index, bits):
    result, bit = index, 1
    while bit <= bits:
        if bits & bit:
            result = result + bit * (1 - 2 * lax.rem(lax.div(index, bit), 2))
        bit *= 2
    return result


def feature_kernel(
    ad_count, group,
    tok, idx, base, down, up, out,
    tok_own, base_all, down_own, packed, gtok, gdown, gup, idx_own, idx_send, gidx,
    ids, acc, part_out, part_in, base_acc, base_in,
    local_sem, chunk_sem, tok_send, tok_recv, down_send, down_recv, up_send, up_recv,
    idx_ssem, idx_rsem, part_send, part_recv, base_send, base_recv,
):
    grp, me, tp = lax.axis_index("grp"), lax.axis_index("ad"), lax.axis_index("tp")
    rows, half_width = tok.shape
    slice_width = half_width // group
    part_width = slice_width // 2
    rank, out_width = up.shape[1], up.shape[2]
    other = 1 - tp
    own_member = lax.rem(me, group)

    def device(slot, cross=0):
        return (grp, flip(me, slot), other if cross else tp)

    def columns(member):
        return pl.ds(pl.multiple_of(member * slice_width, slice_width), slice_width)

    loads = [
        pltpu.make_async_copy(down.at[0], down_own, local_sem.at[0]),
        pltpu.make_async_copy(idx, idx_own, local_sem.at[1]),
        pltpu.make_async_copy(tok, tok_own, local_sem.at[2]),
        pltpu.make_async_copy(tok.at[:, columns(own_member)], gtok.at[0], local_sem.at[3]),
        pltpu.make_async_copy(up.at[0], gup.at[pl.ds(0, rank)], local_sem.at[4]),
    ]
    for load in loads:
        load.start()
    depth = half_width // BASE_CHUNKS
    chunks = [
        pltpu.make_async_copy(
            base.at[pl.ds(c * depth, depth)], base_all.at[pl.ds(c * depth, depth)], chunk_sem.at[c]
        )
        for c in range(BASE_CHUNKS)
    ]
    for chunk in chunks:
        chunk.start()

    barrier = pltpu.get_barrier_semaphore()
    greeted = [(s, 0) for s in range(1, ad_count)] + [(s, 1) for s in range(group)]
    for s, cross in greeted:
        pl.semaphore_signal(barrier, inc=1, device_id=device(s, cross), device_id_type=MESH)
    pl.semaphore_wait(barrier, len(greeted))

    tok_copies = {}
    for s in range(group - 1, 0, -1):
        tok_copies[s] = pltpu.make_async_remote_copy(
            src_ref=tok.at[:, columns(lax.rem(flip(me, s), group))],
            dst_ref=gtok.at[s],
            send_sem=tok_send.at[s], recv_sem=tok_recv.at[s],
            device_id=device(s), device_id_type=MESH,
        )
        tok_copies[s].start()

    loads[0].wait()
    for q in range(group):
        left = down_own[q * slice_width:q * slice_width + part_width, :]
        right = down_own[q * slice_width + part_width:(q + 1) * slice_width, :]
        packed[q] = jnp.concatenate([left, right], axis=1)
    down_copies = {}
    for s in range(ad_count - 1, 0, -1):
        down_copies[s] = pltpu.make_async_remote_copy(
            src_ref=packed.at[lax.rem(flip(me, s), group)],
            dst_ref=gdown.at[:, pl.ds(s * LANES, LANES)],
            send_sem=down_send.at[s], recv_sem=down_recv.at[s],
            device_id=device(s), device_id_type=MESH,
        )
        down_copies[s].start()

    loads[1].wait()
    wide = jnp.broadcast_to(idx_own[...].astype(jnp.float32), (rows, LANES))
    ids[0] = wide.astype(jnp.int32)
    idx_send[...] = wide.T[0:8, :]
    idx_copies = {}
    for s in range(group - 1, 0, -1):
        idx_copies[s] = pltpu.make_async_remote_copy(
            src_ref=idx_send, dst_ref=gidx.at[s],
            send_sem=idx_ssem.at[s], recv_sem=idx_rsem.at[s],
            device_id=device(s), device_id_type=MESH,
        )
        idx_copies[s].start()

    up_copies = {}

    def send_up(source, slot, to):
        up_copies[slot] = pltpu.make_async_remote_copy(
            src_ref=source, dst_ref=gup.at[pl.ds(slot * rank, rank)],
            send_sem=up_send.at[slot], recv_sem=up_recv.at[slot],
            device_id=device(to), device_id_type=MESH,
        )
        up_copies[slot].start()

    for s in list(range(ad_count - 2, 0, -2)) + [1]:
        send_up(up.at[0], s, s)

    gdown[:, 0:LANES] = packed[own_member]

    loads[2].wait()
    base_acc[...] = jnp.zeros_like(base_acc)
    for chunk in chunks:
        chunk.wait()

    @pl.loop(0, BASE_CHUNKS)
    def _(c):
        span = pl.ds(pl.multiple_of(c * depth, depth), depth)
        base_acc[...] += jnp.dot(
            tok_own[:, span], base_all[span, :], preferred_element_type=jnp.float32
        )

    base_copy = pltpu.make_async_remote_copy(
        src_ref=base_acc.at[:, pl.ds(pl.multiple_of(other * out_width, out_width), out_width)],
        dst_ref=base_in,
        send_sem=base_send.at[0], recv_sem=base_recv.at[0],
        device_id=device(0, 1), device_id_type=MESH,
    )
    base_copy.start()

    for s in range(2, ad_count, 2):
        up_copies[s].wait_recv()
        send_up(gup.at[pl.ds(s * rank, rank)], s + 1, 1)

    for s in range(1, group):
        idx_copies[s].wait_recv()
        ids[s] = jnp.broadcast_to(gidx[s][0:1, :], (LANES, rows)).T.astype(jnp.int32)
    loads[3].wait()
    for s in range(1, group):
        tok_copies[s].wait_recv()

    low = lax.broadcasted_iota(jnp.int32, (rows, LANES), 1) < rank
    for p in range(0, ad_count, 2):
        for s in (p, p + 1):
            if s:
                down_copies[s].wait_recv()
        factors = gdown[:, p * LANES:(p + 2) * LANES]
        for m in range(group):
            left = jnp.dot(gtok[m, :, :part_width], factors, preferred_element_type=jnp.float32)
            right = jnp.dot(gtok[m, :, part_width:], factors, preferred_element_type=jnp.float32)
            total = jnp.zeros((rows, LANES), jnp.float32) if p == 0 else acc[m]
            for k in range(2):
                both = jnp.where(
                    low, left[:, k * LANES:(k + 1) * LANES], right[:, k * LANES:(k + 1) * LANES]
                )
                total = jnp.where(ids[m] == flip(me, p + k), both, total)
            acc[m] = total

    part_copies = []
    for m in list(range(group - 1, 0, -1)) + [0]:
        whole = acc[m]
        whole = whole + pltpu.roll(whole, rank, 1)
        part_out[m] = jnp.where(low[:rows // 2], whole[:rows // 2], whole[rows // 2:])
        for cross in (0, 1):
            if m or cross:
                copy = pltpu.make_async_remote_copy(
                    src_ref=part_out.at[m], dst_ref=part_in.at[2 * m + cross],
                    send_sem=part_send.at[2 * m + cross], recv_sem=part_recv.at[2 * m + cross],
                    device_id=device(m, cross), device_id_type=MESH,
                )
                copy.start()
                part_copies.append(copy)

    base_copy.wait_recv()
    kept = base_acc[:, pl.ds(pl.multiple_of(tp * out_width, out_width), out_width)] + base_in[...]
    for s in range(1, ad_count, 2):
        up_copies[s].wait_recv()
    loads[4].wait()

    shrunk = part_out[0]
    for copy in part_copies:
        copy.wait_recv()
    for slot in range(1, 2 * group):
        shrunk = shrunk + part_in[slot]
    turned = pltpu.roll(shrunk, rank, 1)
    low_half = low[:rows // 2]
    spread = jnp.concatenate(
        [jnp.where(low_half, shrunk, turned), jnp.where(low_half, turned, shrunk)], axis=0
    )
    placed = []
    for p in range(0, ad_count, 2):
        named = jnp.where(low, flip(me, p), flip(me, p + 1))
        placed.append(jnp.where(ids[0] == named, spread, 0.0).astype(jnp.bfloat16))
    expanded = jnp.dot(
        jnp.concatenate(placed, axis=1), gup[...], preferred_element_type=jnp.float32
    ).astype(jnp.bfloat16)
    out[...] = (kept + expanded.astype(jnp.float32)).astype(jnp.bfloat16)

    for copies in (tok_copies, down_copies, idx_copies, up_copies):
        for s in copies:
            copies[s].wait_send()
    for copy in part_copies:
        copy.wait_send()
    base_copy.wait_send()


def by_features(ad_count, group, tokens, row_adapter_index, key_base_matrix, down, up):
    rows, half_width = tokens.shape
    key_width = key_base_matrix.shape[1]
    rank, out_width = up.shape[1], up.shape[2]
    slice_width = half_width // group
    bf16, f32, i32 = jnp.bfloat16, jnp.float32, jnp.int32
    dma = pltpu.SemaphoreType.DMA
    return pl.pallas_call(
        functools.partial(feature_kernel, ad_count, group),
        out_shape=jax.ShapeDtypeStruct((rows, out_width), bf16),
        in_specs=[pl.BlockSpec(memory_space=pl.ANY)] * 5,
        out_specs=pl.BlockSpec(memory_space=pltpu.VMEM),
        scratch_shapes=[
            pltpu.VMEM((rows, half_width), bf16),
            pltpu.VMEM((half_width, key_width), bf16),
            pltpu.VMEM((half_width, rank), bf16),
            pltpu.VMEM((group, slice_width // 2, LANES), bf16),
            pltpu.VMEM((group, rows, slice_width), bf16),
            pltpu.VMEM((slice_width // 2, ad_count * LANES), bf16),
            pltpu.VMEM((ad_count * rank, out_width), bf16),
            pltpu.VMEM((rows, 1), i32),
            pltpu.VMEM((8, rows), f32),
            pltpu.VMEM((group, 8, rows), f32),
            pltpu.VMEM((group, rows, LANES), i32),
            pltpu.VMEM((group, rows, LANES), f32),
            pltpu.VMEM((group, rows // 2, LANES), f32),
            pltpu.VMEM((2 * group, rows // 2, LANES), f32),
            pltpu.VMEM((rows, key_width), f32),
            pltpu.VMEM((rows, out_width), f32),
            dma((5,)), dma((BASE_CHUNKS,)),
            dma((group,)), dma((group,)),
            dma((ad_count,)), dma((ad_count,)),
            dma((ad_count,)), dma((ad_count,)),
            dma((group,)), dma((group,)),
            dma((2 * group,)), dma((2 * group,)),
            dma((1,)), dma((1,)),
        ],
        compiler_params=pltpu.CompilerParams(
            collective_id=0, has_side_effects=True, vmem_limit_bytes=48 * 1024 * 1024
        ),
        cost_estimate=pl.CostEstimate(
            flops=2 * rows * half_width * (key_width + 2 * ad_count * rank),
            bytes_accessed=2 * half_width * (key_width + 2 * rows + rank),
            transcendentals=0,
        ),
    )(tokens, row_adapter_index, key_base_matrix, down, up)


def by_rows(ad_count, tokens, row_adapter_index, key_base_matrix, down, up):
    row_count, feature_half = tokens.shape
    capacity = max(2, 2 * row_count // ad_count)
    row_adapter = row_adapter_index[:, 0]
    one_hot = (row_adapter[:, None] == jnp.arange(ad_count, dtype=jnp.int32)[None, :]).astype(
        jnp.int32
    )
    earlier = jnp.cumsum(one_hot, axis=0) - one_hot
    position = row_adapter * capacity + jnp.sum(earlier * one_hot, axis=1)
    outgoing = jnp.zeros((ad_count * capacity, feature_half), jnp.bfloat16).at[position].set(tokens)
    outgoing = outgoing.reshape(ad_count, capacity, feature_half)
    received = lax.all_to_all(outgoing, "ad", split_axis=0, concat_axis=0, tiled=True)
    flat_rows = received.reshape(ad_count * capacity, feature_half)
    shrunk_part = jnp.dot(flat_rows, down[0], preferred_element_type=jnp.float32)
    shrunk = lax.psum(shrunk_part, "tp").astype(jnp.bfloat16)
    expanded = jnp.dot(shrunk, up[0], preferred_element_type=jnp.float32).astype(jnp.bfloat16)
    expanded = expanded.reshape(ad_count, capacity, up.shape[2])
    returned = lax.all_to_all(expanded, "ad", split_axis=0, concat_axis=0, tiled=True)
    base_part = jnp.dot(tokens, key_base_matrix, preferred_element_type=jnp.float32)
    base_half = lax.psum_scatter(base_part, "tp", scatter_dimension=1, tiled=True)
    delta_rows = returned.reshape(ad_count * capacity, up.shape[2])[position]
    return (base_half + delta_rows.astype(jnp.float32)).astype(jnp.bfloat16)


def solution(mesh):
    placed = (
        P(("grp", "ad"), "tp"),
        P(("grp", "ad"), None),
        P("tp", None),
        P(("grp", "ad"), "tp", None),
        P(("grp", "ad"), None, "tp"),
    )
    ad_count = mesh.shape["ad"]
    group = 4
    if ad_count in (group, 2 * group):
        on_device = functools.partial(by_features, ad_count, group)
    else:
        on_device = functools.partial(by_rows, ad_count)
    return jax.shard_map(
        on_device, mesh=mesh, in_specs=placed, out_specs=P(("grp", "ad"), "tp"), check_vma=False
    )
```

time: 112 us -> 55.2 us (0.49)
  waiting for transfers between devices: 65 us -> 0 us
  Pallas kernels: 0 us -> 49.9 us
  starting transfers between devices: 13.2 us -> 0 us
  between operations: 13.2 us -> 0.03 us
  matrix products: 10.1 us -> 0 us
  other arithmetic: 4.07 us -> 0 us
  local copies, waits for them, and re-layouts: 6.55 us -> 4.99 us
    all_to_all x2 -> x0, waiting for transfers between devices: 56.8 us -> none  [the longest x1 47.5 us: on_device(): lax.all_to_all(outgoing, 'ad', split_axis=0, concat_axis=0, tiled=True)]
    pallas_call x0 -> x1, Pallas kernels: none -> 49.9 us  [by_features(): pl.pallas_call(functools.partial(feature_kernel, ad_count, group), out_sh...]
    all_to_all x2 -> x0, starting transfers between devices: 13.1 us -> none  [the longest x1 7.28 us: on_device(): lax.all_to_all(outgoing, 'ad', split_axis=0, concat_axis=0, tiled=True)]
    dot_general x2 -> x0, matrix products: 10.1 us -> none  [the longest x1 5.41 us: on_device(): jnp.dot(tokens, key_base_matrix, preferred_element_type=jnp.float32)]
    all_gather x2 -> x0, waiting for transfers between devices: 7.38 us -> none  [the longest x1 7.36 us: on_device(): whole_rows = lax.all_gather(flat_rows, 'tp', axis=1, tiled=True)]
    scatter x1 -> x0, local copies, waits for them, and re-layouts: 4.37 us -> none  [on_device(): jnp.zeros((ad_count * capacity, feature_half), jnp.bfloat16).at[position]]
    unnamed x6 -> x7, local copies, waits for them, and re-layouts: 1.33 us -> 4.99 us
    convert_element_type x2 -> x0, other arithmetic: 2.4 us -> none  [the longest x1 1.63 us: on_device(): return (base_half + delta_rows.astype(jnp.float32)).astype(jnp.bfloat16)]
  transfers between devices with their start and end apart: 5 -> 0, of which waited for: 3 -> 0; matrix products, arithmetic and copies ran while one was open for 10% -> 0% of each run, Pallas kernels for 0% -> 0%
where the time goes in v1:
time: 55.2 us; the launch traced here: 55 us
  Pallas kernels  49.9 us (90%)
  local copies, waits for them, and re-layouts  4.99 us (9%)
    pallas_call x1, Pallas kernels, by_features(): pl.pallas_call(functools.partial(feature_kernel, ad_count, group), out_sh...  49.9 us
    unnamed x7, local copies, waits for them, and re-layouts  4.99 us

profile of v1, /device:TPU:0, one launch (start us, length us, event | category | flops | bytes accessed | tf_op | source)
XLA Modules:
  0.0 55.0 jit_solution(330202532626537012)
XLA Ops:
  0.0 0.8 %copy.6.idx = s32[128,1]{1,0:T(8,128)S(1)} copy(s32[128,1]{0,1:T(1,128)} %param.6) | data formatting | bytes 1024 | tf_op args[1]
  0.8 1.5 %copy.7.down = bf16[1,4096,64]{2,1,0:T(8,128)(2,1)S(1)} copy(bf16[1,4096,64]{1,2,0:T(8,128)(2,1)} %param.8) | data formatting | bytes 1048576 | tf_op args[3]
  2.3 0.0 copy-start
  2.3 1.2 %copy-done = bf16[128,4096]{1,0:T(8,128)(2,1)S(1)} copy-done((bf16[128,4096]{1,0:T(8,128)(2,1)S(1)}, bf16[128,4096]{1,0:T(8,128)(2,1)}, u32[]{:S(2)}) %copy-start) | copy-done | bytes 1048600
  3.5 0.0 copy-start.1
  3.5 0.8 %copy-done.1 = bf16[1,64,512]{2,1,0:T(8,128)(2,1)S(1)} copy-done((bf16[1,64,512]{2,1,0:T(8,128)(2,1)S(1)}, bf16[1,64,512]{2,1,0:T(8,128)(2,1)}, u32[]{:S(2)}) %copy-start.1) | copy-done | bytes 65560
  4.4 49.9 %shard_map.55 = bf16[128,512]{1,0:T(8,128)(2,1)S(1)} custom-call(bf16[128,4096]{1,0:T(8,128)(2,1)S(1)} %copy-done, s32[128,1]{1,0:T(8,128)S(1)} %copy.6.idx, bf16[4096,1024]{1,0:T(8,128)(2,1)} %base.1, bf16[1,4096,64]{2,1,0:T(8,128)(2,1)S(1)} %copy.7.down, bf16[1,64,512]{2,1,0:T(8,128)(2,1)S(1)} %copy-done.1), custom_call_target="tpu_custom_call" | custom-call | flops 2147483648 | bytes 11010048 | tf_op jit(solution)/shard_map/pallas_call | solution.py:227
  54.3 0.7 %copy.9 = bf16[128,512]{1,0:T(8,128)(2,1)} copy(bf16[128,512]{1,0:T(8,128)(2,1)S(1)} %shard_map.55) | data formatting | bytes 262144
Async XLA Ops:
  2.3 1.2 %copy-start = (bf16[128,4096]{1,0:T(8,128)(2,1)S(1)}, bf16[128,4096]{1,0:T(8,128)(2,1)}, u32[]{:S(2)}) copy-start(bf16[128,4096]{1,0:T(8,128)(2,1)} %tok.1) | copy-start | bytes 3145732
  3.5 0.8 %copy-start.1 = (bf16[1,64,512]{2,1,0:T(8,128)(2,1)S(1)}, bf16[1,64,512]{2,1,0:T(8,128)(2,1)}, u32[]{:S(2)}) copy-start(bf16[1,64,512]{2,1,0:T(8,128)(2,1)} %up.1) | copy-start | bytes 196612

commit v2 on v1

--- a/solution.py
+++ b/solution.py
@@ -10,6 +10,7 @@
 MESH = pl.DeviceIdType.MESH
 LANES = 128
 BASE_CHUNKS = 8
+FACTORS = 4
 
 
 def flip(index, bits):
@@ -24,7 +25,7 @@
 def feature_kernel(
     ad_count, group,
     tok, idx, base, down, up, out,
-    tok_own, base_all, down_own, packed, gtok, gdown, gup, idx_own, idx_send, gidx,
+    tok_own, base_all, gtok, gdown, gup, gidx,
     ids, acc, part_out, part_in, base_acc, base_in,
     local_sem, chunk_sem, tok_send, tok_recv, down_send, down_recv, up_send, up_recv,
     idx_ssem, idx_rsem, part_send, part_recv, base_send, base_recv,
@@ -32,7 +33,6 @@
     grp, me, tp = lax.axis_index("grp"), lax.axis_index("ad"), lax.axis_index("tp")
     rows, half_width = tok.shape
     slice_width = half_width // group
-    part_width = slice_width // 2
     rank, out_width = up.shape[1], up.shape[2]
     other = 1 - tp
     own_member = lax.rem(me, group)
@@ -44,8 +44,10 @@
         return pl.ds(pl.multiple_of(member * slice_width, slice_width), slice_width)
 
     loads = [
-        pltpu.make_async_copy(down.at[0], down_own, local_sem.at[0]),
-        pltpu.make_async_copy(idx, idx_own, local_sem.at[1]),
+        pltpu.make_async_copy(
+            down.at[0, :, columns(own_member)], gdown.at[pl.ds(0, rank)], local_sem.at[0]
+        ),
+        pltpu.make_async_copy(idx, gidx.at[0], local_sem.at[1]),
         pltpu.make_async_copy(tok, tok_own, local_sem.at[2]),
         pltpu.make_async_copy(tok.at[:, columns(own_member)], gtok.at[0], local_sem.at[3]),
         pltpu.make_async_copy(up.at[0], gup.at[pl.ds(0, rank)], local_sem.at[4]),
@@ -78,29 +80,20 @@
         )
         tok_copies[s].start()
 
-    loads[0].wait()
-    for q in range(group):
-        left = down_own[q * slice_width:q * slice_width + part_width, :]
-        right = down_own[q * slice_width + part_width:(q + 1) * slice_width, :]
-        packed[q] = jnp.concatenate([left, right], axis=1)
     down_copies = {}
     for s in range(ad_count - 1, 0, -1):
         down_copies[s] = pltpu.make_async_remote_copy(
-            src_ref=packed.at[lax.rem(flip(me, s), group)],
-            dst_ref=gdown.at[:, pl.ds(s * LANES, LANES)],
+            src_ref=down.at[0, :, columns(lax.rem(flip(me, s), group))],
+            dst_ref=gdown.at[pl.ds(s * rank, rank)],
             send_sem=down_send.at[s], recv_sem=down_recv.at[s],
             device_id=device(s), device_id_type=MESH,
         )
         down_copies[s].start()
 
-    loads[1].wait()
-    wide = jnp.broadcast_to(idx_own[...].astype(jnp.float32), (rows, LANES))
-    ids[0] = wide.astype(jnp.int32)
-    idx_send[...] = wide.T[0:8, :]
     idx_copies = {}
     for s in range(group - 1, 0, -1):
         idx_copies[s] = pltpu.make_async_remote_copy(
-            src_ref=idx_send, dst_ref=gidx.at[s],
+            src_ref=idx, dst_ref=gidx.at[s],
             send_sem=idx_ssem.at[s], recv_sem=idx_rsem.at[s],
             device_id=device(s), device_id_type=MESH,
         )
@@ -119,8 +112,6 @@
     for s in list(range(ad_count - 2, 0, -2)) + [1]:
         send_up(up.at[0], s, s)
 
-    gdown[:, 0:LANES] = packed[own_member]
-
     loads[2].wait()
     base_acc[...] = jnp.zeros_like(base_acc)
     for chunk in chunks:
@@ -145,28 +136,30 @@
         up_copies[s].wait_recv()
         send_up(gup.at[pl.ds(s * rank, rank)], s + 1, 1)
 
-    for s in range(1, group):
-        idx_copies[s].wait_recv()
-        ids[s] = jnp.broadcast_to(gidx[s][0:1, :], (LANES, rows)).T.astype(jnp.int32)
+    loads[1].wait()
+    for s in range(group):
+        if s:
+            idx_copies[s].wait_recv()
+        ids[s] = jnp.broadcast_to(gidx[s], (LANES, rows)).astype(jnp.float32).T.astype(jnp.int32)
+    loads[0].wait()
     loads[3].wait()
     for s in range(1, group):
         tok_copies[s].wait_recv()
 
     low = lax.broadcasted_iota(jnp.int32, (rows, LANES), 1) < rank
-    for p in range(0, ad_count, 2):
-        for s in (p, p + 1):
+    for p in range(0, ad_count, FACTORS):
+        for s in range(p, p + FACTORS):
             if s:
                 down_copies[s].wait_recv()
-        factors = gdown[:, p * LANES:(p + 2) * LANES]
+        factors = gdown[p * rank:(p + FACTORS) * rank, :]
         for m in range(group):
-            left = jnp.dot(gtok[m, :, :part_width], factors, preferred_element_type=jnp.float32)
-            right = jnp.dot(gtok[m, :, part_width:], factors, preferred_element_type=jnp.float32)
+            product = lax.dot_general(
+                gtok[m], factors, (((1,), (1,)), ((), ())), preferred_element_type=jnp.float32
+            )
             total = jnp.zeros((rows, LANES), jnp.float32) if p == 0 else acc[m]
-            for k in range(2):
-                both = jnp.where(
-                    low, left[:, k * LANES:(k + 1) * LANES], right[:, k * LANES:(k + 1) * LANES]
-                )
-                total = jnp.where(ids[m] == flip(me, p + k), both, total)
+            for k in range(0, FACTORS, 2):
+                named = jnp.where(low, flip(me, p + k), flip(me, p + k + 1))
+                total = jnp.where(ids[m] == named, product[:, k * rank:(k + 2) * rank], total)
             acc[m] = total
 
     part_copies = []
@@ -232,14 +225,10 @@
         scratch_shapes=[
             pltpu.VMEM((rows, half_width), bf16),
             pltpu.VMEM((half_width, key_width), bf16),
-            pltpu.VMEM((half_width, rank), bf16),
-            pltpu.VMEM((group, slice_width // 2, LANES), bf16),
             pltpu.VMEM((group, rows, slice_width), bf16),
-            pltpu.VMEM((slice_width // 2, ad_count * LANES), bf16),
+            pltpu.VMEM((ad_count * rank, slice_width), bf16),
             pltpu.VMEM((ad_count * rank, out_width), bf16),
-            pltpu.VMEM((rows, 1), i32),
-            pltpu.VMEM((8, rows), f32),
-            pltpu.VMEM((group, 8, rows), f32),
+            pltpu.VMEM((group, 1, rows), i32),
             pltpu.VMEM((group, rows, LANES), i32),
             pltpu.VMEM((group, rows, LANES), f32),
             pltpu.VMEM((group, rows // 2, LANES), f32),
@@ -255,14 +244,14 @@
             dma((1,)), dma((1,)),
         ],
         compiler_params=pltpu.CompilerParams(
-            collective_id=0, has_side_effects=True, vmem_limit_bytes=48 * 1024 * 1024
+            collective_id=0, has_side_effects=True, vmem_limit_bytes=63 * 1024 * 1024
         ),
         cost_estimate=pl.CostEstimate(
             flops=2 * rows * half_width * (key_width + 2 * ad_count * rank),
             bytes_accessed=2 * half_width * (key_width + 2 * rows + rank),
             transcendentals=0,
         ),
-    )(tokens, row_adapter_index, key_base_matrix, down, up)
+    )(tokens, row_adapter_index.reshape(1, rows), key_base_matrix, jnp.swapaxes(down, 1, 2), up)
 
 
 def by_rows(ad_count, tokens, row_adapter_index, key_base_matrix, down, up):

time: 55.2 us -> 51.7 us (0.937)
  local copies, waits for them, and re-layouts: 4.99 us -> 1.57 us
    unnamed x7 -> x1, local copies, waits for them, and re-layouts: 4.99 us -> 1.57 us
where the time goes in v2:
time: 51.7 us; the launch traced here: 51.6 us
  Pallas kernels  50 us (97%)
  local copies, waits for them, and re-layouts  1.57 us (3%)
    pallas_call x1, Pallas kernels, by_features(): pl.pallas_call(functools.partial(feature_kernel, ad_count, group), out_sh...  50 us
    unnamed x1, local copies, waits for them, and re-layouts  1.57 us

profile of v2, /device:TPU:0, one launch (start us, length us, event | category | flops | bytes accessed | tf_op | source)
XLA Modules:
  0.0 51.6 jit_solution(12867603772430906260)
XLA Ops:
  0.0 50.0 %shard_map.55 = bf16[128,512]{1,0:T(8,128)(2,1)} custom-call(bf16[128,4096]{1,0:T(8,128)(2,1)} %tok.1, s32[1,128]{1,0:T(1,128)} %bitcast.3, bf16[4096,1024]{1,0:T(8,128)(2,1)} %base.1, bf16[1,64,4096]{2,1,0:T(8,128)(2,1)} %bitcast.2, bf16[1,64,512]{2,1,0:T(8,128)(2,1)} %up.1), custom_call_target="tpu_custom_call" | custom-call | flops 2147483648 | bytes 11010048 | tf_op jit(solution)/shard_map/pallas_call | solution.py:220
  50.0 1.6 %copy.7 = bf16[128,512]{1,0:T(8,128)(2,1)} copy(bf16[128,512]{1,0:T(8,128)(2,1)} %shard_map.55) | data formatting | bytes 262144

commit v3 on v2

--- a/solution.py
+++ b/solution.py
@@ -10,7 +10,7 @@
 MESH = pl.DeviceIdType.MESH
 LANES = 128
 BASE_CHUNKS = 8
-FACTORS = 4
+FACTORS = 2
 
 
 def flip(index, bits):
@@ -78,7 +78,6 @@
             send_sem=tok_send.at[s], recv_sem=tok_recv.at[s],
             device_id=device(s), device_id_type=MESH,
         )
-        tok_copies[s].start()
 
     down_copies = {}
     for s in range(ad_count - 1, 0, -1):
@@ -88,7 +87,6 @@
             send_sem=down_send.at[s], recv_sem=down_recv.at[s],
             device_id=device(s), device_id_type=MESH,
         )
-        down_copies[s].start()
 
     idx_copies = {}
     for s in range(group - 1, 0, -1):
@@ -97,7 +95,6 @@
             send_sem=idx_ssem.at[s], recv_sem=idx_rsem.at[s],
             device_id=device(s), device_id_type=MESH,
         )
-        idx_copies[s].start()
 
     up_copies = {}
 
@@ -107,10 +104,22 @@
             send_sem=up_send.at[slot], recv_sem=up_recv.at[slot],
             device_id=device(to), device_id_type=MESH,
         )
-        up_copies[slot].start()
-
-    for s in list(range(ad_count - 2, 0, -2)) + [1]:
+
+    direct = [1] + list(range(2, ad_count, 2))
+    for s in direct:
         send_up(up.at[0], s, s)
+
+    near, far = list(range(1, group)), list(range(group, ad_count))
+    for s in near:
+        idx_copies[s].start()
+    for s in direct:
+        up_copies[s].start()
+    for s in sorted(far, key=lambda s: (s % 2, s)):
+        down_copies[s].start()
+    for s in near:
+        tok_copies[s].start()
+    for s in near:
+        down_copies[s].start()
 
     loads[2].wait()
     base_acc[...] = jnp.zeros_like(base_acc)
@@ -135,6 +144,7 @@
     for s in range(2, ad_count, 2):
         up_copies[s].wait_recv()
         send_up(gup.at[pl.ds(s * rank, rank)], s + 1, 1)
+        up_copies[s + 1].start()
 
     loads[1].wait()
     for s in range(group):

time: 51.7 us -> 48.6 us (0.940)
  Pallas kernels: 50 us -> 46.9 us
    pallas_call x1, Pallas kernels: 50 us -> 46.9 us  [by_features(): pl.pallas_call(functools.partial(feature_kernel, ad_count, group), out_sh...]
where the time goes in v3:
time: 48.6 us; the launch traced here: 48.5 us
  Pallas kernels  46.9 us (97%)
  local copies, waits for them, and re-layouts  1.57 us (3%)
    pallas_call x1, Pallas kernels, by_features(): pl.pallas_call(functools.partial(feature_kernel, ad_count, group), out_sh...  46.9 us
    unnamed x1, local copies, waits for them, and re-layouts  1.57 us

profile of v3, /device:TPU:0, one launch (start us, length us, event | category | flops | bytes accessed | tf_op | source)
XLA Modules:
  0.0 48.5 jit_solution(8055584133596726383)
XLA Ops:
  0.0 46.9 %shard_map.55 = bf16[128,512]{1,0:T(8,128)(2,1)} custom-call(bf16[128,4096]{1,0:T(8,128)(2,1)} %tok.1, s32[1,128]{1,0:T(1,128)} %bitcast.3, bf16[4096,1024]{1,0:T(8,128)(2,1)} %base.1, bf16[1,64,4096]{2,1,0:T(8,128)(2,1)} %bitcast.2, bf16[1,64,512]{2,1,0:T(8,128)(2,1)} %up.1), custom_call_target="tpu_custom_call" | custom-call | flops 2147483648 | bytes 11010048 | tf_op jit(solution)/shard_map/pallas_call | solution.py:230
  46.9 1.6 %copy.7 = bf16[128,512]{1,0:T(8,128)(2,1)} copy(bf16[128,512]{1,0:T(8,128)(2,1)} %shard_map.55) | data formatting | bytes 262144

commit v4 on v3

--- a/solution.py
+++ b/solution.py
@@ -42,6 +42,11 @@
 
     def columns(member):
         return pl.ds(pl.multiple_of(member * slice_width, slice_width), slice_width)
+
+    barrier = pltpu.get_barrier_semaphore()
+    greeted = [(s, 0) for s in range(1, ad_count)] + [(s, 1) for s in range(group)]
+    for s, cross in greeted:
+        pl.semaphore_signal(barrier, inc=1, device_id=device(s, cross), device_id_type=MESH)
 
     loads = [
         pltpu.make_async_copy(
@@ -61,13 +66,7 @@
         )
         for c in range(BASE_CHUNKS)
     ]
-    for chunk in chunks:
-        chunk.start()
-
-    barrier = pltpu.get_barrier_semaphore()
-    greeted = [(s, 0) for s in range(1, ad_count)] + [(s, 1) for s in range(group)]
-    for s, cross in greeted:
-        pl.semaphore_signal(barrier, inc=1, device_id=device(s, cross), device_id_type=MESH)
+
     pl.semaphore_wait(barrier, len(greeted))
 
     tok_copies = {}
@@ -121,6 +120,8 @@
     for s in near:
         down_copies[s].start()
 
+    for chunk in chunks:
+        chunk.start()
     loads[2].wait()
     base_acc[...] = jnp.zeros_like(base_acc)
     for chunk in chunks:

time: 48.6 us -> 48.6 us (level)
  no operation moved by 1% of the time
where the time goes in v4:
time: 48.6 us; the launch traced here: 48.4 us
  Pallas kernels  46.9 us (97%)
  local copies, waits for them, and re-layouts  1.57 us (3%)
    pallas_call x1, Pallas kernels, by_features(): pl.pallas_call(functools.partial(feature_kernel, ad_count, group), out_sh...  46.9 us
    unnamed x1, local copies, waits for them, and re-layouts  1.57 us

profile of v4, /device:TPU:0, one launch (start us, length us, event | category | flops | bytes accessed | tf_op | source)
XLA Modules:
  0.0 48.4 jit_solution(4672049422995134509)
XLA Ops:
  0.0 46.9 %shard_map.55 = bf16[128,512]{1,0:T(8,128)(2,1)} custom-call(bf16[128,4096]{1,0:T(8,128)(2,1)} %tok.1, s32[1,128]{1,0:T(1,128)} %bitcast.3, bf16[4096,1024]{1,0:T(8,128)(2,1)} %base.1, bf16[1,64,4096]{2,1,0:T(8,128)(2,1)} %bitcast.2, bf16[1,64,512]{2,1,0:T(8,128)(2,1)} %up.1), custom_call_target="tpu_custom_call" | custom-call | flops 2147483648 | bytes 11010048 | tf_op jit(solution)/shard_map/pallas_call | solution.py:231
  46.9 1.6 %copy.7 = bf16[128,512]{1,0:T(8,128)(2,1)} copy(bf16[128,512]{1,0:T(8,128)(2,1)} %shard_map.55) | data formatting | bytes 262144
